TPU v7x, 32 devices: a whole 2x2x4 slice. The times are simulated.
32 devices in a mesh: tok: 8 (over y, x, core), blk: 4 (over z).
Axes of the slice: x: 2, y: 2, z: 4, core: 2. Of those that a mesh axis runs over, the one named last changes fastest.
Arguments:
- attn_out: bfloat16 [4096, 1536], P(('tok', 'blk')), may hold values from -6 to 6
- resid: bfloat16 [4096, 1536], P(('tok', 'blk')), may hold values from -6 to 6
- w_o: bfloat16 [1536, 1536], replicated, may hold values from -0.15625 to 0.15625
- norm1_gain: float32 [1536], replicated, may hold values from 0.1 to 1.9
- router_w: float32 [1536, 40], replicated, may hold values from -32 to 32
- route_slot: int32 [4096, 8], P(('tok', 'blk')), may hold values from 0 to 63, all different within a row; in each aligned block of 128 rows (0 to 127, 128 to 255, ...) at most 32 rows name the same one
- slot_expert: int32 [64], replicated, may hold values from 0 to 39, as said below
- keep: int32 [4096], P(('tok', 'blk')), may hold values 0 or 1
- w_gate: bfloat16 [64, 1536, 512], P('tok', 'blk'), may hold values from -0.15625 to 0.15625
- w_up: bfloat16 [64, 1536, 512], P('tok', 'blk'), may hold values from -0.15625 to 0.15625
- w_down: bfloat16 [64, 1536, 512], P('tok', 'blk'), may hold values from -0.25 to 0.25
- norm2_gain: float32 [1536], replicated, may hold values from 0.1 to 1.9
Outputs:
- layer_out: bfloat16 [4096, 1536], P(('tok', 'blk'))
Inputs may be any that keep to these rules, and one draw needn't show every extreme that they name: `route_slot`: each row names 8 different slots; among the 128 rows of one device (aligned blocks of rows), no slot is named more than 32 times, a bound that some block reaches. `slot_expert`: every expert is named by one slot or more.
All inputs are finite; a program needn't handle non-finite values. No bound on the sum of `keep` on one device may be relied on, other than what follows from the above.
Results may differ from a plain program's by a relative error of at most 0.0099.
Values may be sent and summed in bfloat16 or wider, within the bound.
A program may use at most 128 MiB of HBM per device.

v0:
```python
import jax
import jax.numpy as jnp
from jax import lax
from jax.sharding import PartitionSpec as P

eps = 1e-05


def rms_scale(values, gain):
    mean_sq = jnp.mean(values * values, axis=-1, keepdims=True)
    return values * lax.rsqrt(mean_sq + eps) * gain


def body(
    attn_out,
    resid,
    w_o,
    norm1_gain,
    router_w,
    route_slot,
    slot_expert,
    keep,
    w_gate,
    w_up,
    w_down,
    norm2_gain,
):
    rows, top = route_slot.shape
    width = resid.shape[1]
    slot_dev = w_gate.shape[0]
    groups = lax.axis_size("tok")
    slots = slot_dev * groups
    cap = max(2, 2 * rows * top // slots)
    hidden_state = resid.astype(jnp.float32) + jnp.dot(
        attn_out, w_o, preferred_element_type=jnp.float32
    )
    normed = rms_scale(hidden_state, norm1_gain).astype(jnp.bfloat16)
    logits = jnp.dot(normed.astype(jnp.float32), router_w, precision=lax.Precision.HIGHEST)
    slot_hits = route_slot[:, :, None] == jnp.arange(slots, dtype=jnp.int32)[None, None, :]
    expert_of = jnp.sum(jnp.where(slot_hits, slot_expert[None, None, :], 0), axis=-1)
    expert_hits = (
        expert_of[:, :, None] == jnp.arange(router_w.shape[1], dtype=jnp.int32)[None, None, :]
    )
    chosen = jnp.sum(jnp.where(expert_hits, logits[:, None, :], jnp.float32(0.0)), axis=-1)
    probs = jax.nn.softmax(chosen, axis=-1)
    live_rows = keep > 0
    live = jnp.repeat(live_rows, top)
    flat_hits = (slot_hits.reshape(rows * top, slots) & live[:, None]).astype(jnp.int32)
    before = jnp.cumsum(flat_hits, axis=0) - flat_hits
    position = jnp.sum(before * flat_hits, axis=1)
    flat_slot = route_slot.reshape(-1)
    owner = flat_slot // slot_dev
    local = flat_slot % slot_dev
    target_row = owner * cap + position
    target_local = jnp.where(live, local, slot_dev)
    token_index = jnp.arange(rows * top, dtype=jnp.int32) // top
    outgoing = jnp.zeros((slot_dev, groups * cap, width), jnp.bfloat16)
    outgoing = outgoing.at[target_local, target_row].set(normed[token_index], mode="drop")
    received = lax.all_to_all(outgoing, "tok", split_axis=1, concat_axis=1, tiled=True)
    gate_part = jnp.einsum(
        "snd,sdf->snf",
        received,
        lax.all_gather(w_gate, "blk", axis=1, tiled=True),
        preferred_element_type=jnp.float32,
    )
    up_part = jnp.einsum(
        "snd,sdf->snf",
        received,
        lax.all_gather(w_up, "blk", axis=1, tiled=True),
        preferred_element_type=jnp.float32,
    )
    act = (jax.nn.silu(gate_part) * up_part).astype(jnp.bfloat16)
    expert_y = jnp.einsum(
        "snf,sdf->snd",
        act,
        lax.all_gather(w_down, "blk", axis=1, tiled=True),
        preferred_element_type=jnp.float32,
    ).astype(jnp.bfloat16)
    returned = lax.all_to_all(expert_y, "tok", split_axis=1, concat_axis=1, tiled=True)
    picked = returned[local, target_row]
    scale = probs.reshape(-1) * live.astype(jnp.float32)
    moe = jnp.sum((picked.astype(jnp.float32) * scale[:, None]).reshape(rows, top, width), axis=1)
    mixed = hidden_state + moe
    return rms_scale(mixed, norm2_gain).astype(jnp.bfloat16)


def solution(mesh):
    placed = (
        P(("tok", "blk"), None),
        P(("tok", "blk"), None),
        P(),
        P(),
        P(),
        P(("tok", "blk"), None),
        P(),
        P(("tok", "blk")),
        P("tok", "blk", None),
        P("tok", "blk", None),
        P("tok", "blk", None),
        P(),
    )
    return jax.shard_map(
        body, mesh=mesh, in_specs=placed, out_specs=P(("tok", "blk"), None), check_vma=False
    )
```

profile of v0, /device:TPU:0, one launch (start us, length us, event | category | flops | bytes accessed | tf_op | source)
XLA Modules:
  0.0 814.7 jit_solution(9839438439906426216)
XLA Ops:
  6.5 0.0 copy-start
  6.5 0.0 copy-start.10
  6.5 0.0 copy-start.9
  6.5 0.0 copy-start.3
  6.6 0.0 all-gather.6.cloned.1.call-start
  6.6 0.7 all-gather.6.cloned.1.call-update
  7.3 0.0 all-gather.4.cloned.1.call-start
  7.3 0.7 all-gather.4.cloned.1.call-update
  8.0 0.0 copy-start.6
  8.1 0.0 all-gather.8.cloned.1.call-start
  8.1 0.7 all-gather.8.cloned.1.call-update
  8.8 0.0 copy-done.5
  8.8 0.1 copy.46
  8.9 0.1 eq.51
  9.0 0.1 eq.47
  9.1 0.1 reshape.287
  9.2 0.0 copy-done.11
  9.2 0.1 broadcast_in_dim.58
  9.3 0.1 broadcast_in_dim.37.clone
  9.4 0.1 and.78
  9.5 0.1 reshape.286
  9.6 0.1 broadcast_in_dim.59
  9.7 0.1 broadcast_in_dim.60
  9.8 18.0 %reduce-window.6 = s32[64,8,128]{2,1,0:T(8,128)S(1)} reduce-window(s32[64,8,128]{2,1,0:T(8,128)S(1)} %fusion.18, s32[]{:T(128)} %constant.54.clone.1), window={size=1x1x128 pad=0_0x0_0x127_0}, to_apply=%region_0.0 | reduce-window | flops 8323072 | bytes 524292 | tf_op jit(solution)/shard_map/reduce-window
  27.8 0.1 slice.12
  28.0 0.1 copy.50
  28.2 0.1 copy.51
  28.3 0.1 broadcast_add_fusion
  28.4 0.1 fusion.15
  28.5 0.1 fusion.21
  28.6 0.0 copy-done.10
  28.6 0.1 multiply_reduce_fusion.2
  28.7 0.0 copy-done.9
  28.7 0.1 and_reduce_fusion
  28.8 0.0 copy-done
  28.8 0.0 copy-done.3
  28.8 3.2 multiply_reduce_fusion.1
  32.0 0.9 copy-done.2
  32.9 0.0 copy-done.6
  32.9 0.1 multiply_convert_fusion.3
  33.0 20.0 %scatter_custom_fusion = bf16[2048,1536]{1,0:T(8,128)(2,1)} fusion(s32[1024]{0:T(1024)S(1)} %get-tuple-element.13, bf16[128,1536]{1,0:T(8,128)(2,1)S(1)} %multiply_convert_fusion.3, s32[1024]{0:T(1024)S(1)} %get-tuple-element.12, bf16[]{:T(256)} %constant.53.clone.1), kind=kCustom, calls=%fused_computation.11 | custom fusion | bytes 6291458
  53.1 6.3 copy.52
  59.4 76.6 %all_to_all.10 = bf16[8,256,1536]{2,0,1:T(8,128)(2,1)} all-to-all(bf16[8,256,1536]{2,0,1:T(8,128)(2,1)S(1)} %copy.52), channel_id=1, replica_groups=mesh['tok'=8,'blk'=4] {'tok'}, dimensions={1} | all-to-all | bytes 12582912 | tf_op jit(solution)/shard_map/all_to_all | solution.py:59
  136.0 94.0 %all-gather.6.cloned.1.call-done = bf16[8,1536,512]{2,1,0:T(8,128)(2,1)} async-done(((bf16[8,384,512]{2,1,0:T(8,128)(2,1)}), bf16[8,1536,512]{2,1,0:T(8,128)(2,1)}) %all-gather.6.cloned.1.call-update) | async-done | bytes 12582928 | tf_op jit(solution)/shard_map/all_gather | solution.py:69
  230.0 12.8 %fusion.1 = f32[8,256,512]{2,1,0:T(8,128)} fusion(bf16[8,1536,512]{2,1,0:T(8,128)(2,1)} %all-gather.6.cloned.1.call-done, bf16[8,256,1536]{2,0,1:T(8,128)(2,1)} %all_to_all.10), kind=kOutput, calls=%fused_computation.5 | convolution fusion | flops 3221225472 | bytes 23068672 | tf_op jit(solution)/shard_map/snd,sdf->snf/dot_general | solution.py:66
  242.7 205.3 %all-gather.4.cloned.1.call-done = bf16[8,1536,512]{2,1,0:T(8,128)(2,1)} async-done(((bf16[8,384,512]{2,1,0:T(8,128)(2,1)}), bf16[8,1536,512]{2,1,0:T(8,128)(2,1)}) %all-gather.4.cloned.1.call-update) | async-done | bytes 12582928 | tf_op jit(solution)/shard_map/all_gather | solution.py:63
  448.0 218.0 %all-gather.8.cloned.1.call-done = bf16[8,1536,512]{2,1,0:T(8,128)(2,1)} async-done(((bf16[8,384,512]{2,1,0:T(8,128)(2,1)}), bf16[8,1536,512]{2,1,0:T(8,128)(2,1)}) %all-gather.8.cloned.1.call-update) | async-done | bytes 12582928 | tf_op jit(solution)/shard_map/all_gather | solution.py:76
  666.0 25.3 %convolution_convert_fusion = bf16[8,256,1536]{2,1,0:T(8,128)(2,1)} fusion(bf16[8,1536,512]{2,1,0:T(8,128)(2,1)} %all-gather.8.cloned.1.call-done, f32[8,256,512]{2,1,0:T(8,128)} %fusion.1, bf16[8,1536,512]{2,1,0:T(8,128)(2,1)} %all-gather.4.cloned.1.call-done, bf16[8,256,1536]{2,0,1:T(8,128)(2,1)} %all_to_all.10), kind=kOutput, calls=%fused_computation.9 | convolution fusion | flops 6451888128 | bytes 41943040 | tf_op jit(solution)/shard_map/snf,sdf->snd/dot_general | solution.py:73
  691.4 8.9 %copy.55 = bf16[8,256,1536]{2,0,1:T(8,128)(2,1)} copy(bf16[8,256,1536]{2,1,0:T(8,128)(2,1)} %convolution_convert_fusion) | data formatting | bytes 12582912 | tf_op jit(solution)/shard_map/convert_element_type | solution.py:78
  700.3 4.9 all-to-all-start.1
  705.2 0.0 copy-done.8
  705.2 0.1 select_reduce_fusion
  705.3 0.0 copy-done.4
  705.3 0.5 fusion.24
  705.9 0.7 copy.57
  706.6 70.1 %all-to-all-done.1 = bf16[8,256,1536]{2,0,1:T(8,128)(2,1)} async-done(((bf16[8,256,1536]{2,0,1:T(8,128)(2,1)}), bf16[8,256,1536]{2,0,1:T(8,128)(2,1)}, u32[]{:S(2)}, u32[]{:S(2)}) %all-to-all-start.1) | async-done | bytes 6291488 | tf_op jit(solution)/shard_map/all_to_all | solution.py:79
  776.8 7.5 copy.56
  784.2 17.8 %gather_fusion = bf16[1024,1536]{1,0:T(8,128)(2,1)S(1)} fusion(bf16[8,256,1536]{2,1,0:T(8,128)(2,1)} %copy.56, s32[1024]{0:T(1024)S(1)} %bitcast.32), kind=kCustom, calls=%fused_computation.1 | custom fusion | bytes 6299648 | tf_op jit(solution)/shard_map/gather | solution.py:80
  802.0 0.0 copy-start.7
  802.0 3.7 fusion
  805.7 1.3 multiply_reduce_fusion
  807.1 0.0 copy-done.7
  807.1 0.9 multiply_convert_fusion.2
  808.0 0.0 copy-done.1
  (19 shorter events, 0.2 us)
Async XLA Ops:
  6.5 22.2 %copy-start = (bf16[128,1536]{1,0:T(8,128)(2,1)S(1)}, bf16[128,1536]{1,0:T(8,128)(2,1)}, u32[]{:S(2)}) copy-start(bf16[128,1536]{1,0:T(8,128)(2,1)} %param.12) | copy-start | bytes 1179652
  6.5 22.0 %copy-start.10 = (s32[2]{0:T(128)S(1)}, s32[2]{0:T(128)}, u32[]{:S(2)}) copy-start(s32[2]{0:T(128)} %constant.68) | copy-start | bytes 28
  6.5 22.1 %copy-start.9 = (s32[2]{0:T(128)S(1)}, s32[2]{0:T(128)}, u32[]{:S(2)}) copy-start(s32[2]{0:T(128)} %constant.71) | copy-start | bytes 28
  6.5 2.2 copy-start.5
  6.5 2.6 copy-start.11
  6.5 22.2 %copy-start.3 = (bf16[128,1536]{1,0:T(8,128)(2,1)S(1)}, bf16[128,1536]{1,0:T(8,128)(2,1)}, u32[]{:S(2)}) copy-start(bf16[128,1536]{1,0:T(8,128)(2,1)} %param.13) | copy-start | bytes 1179652
  6.6 223.4 %all-gather.6.cloned.1.call-start = ((), (), s32[]{:S(2)}) async-start(), calls=%async_computation.3 | async-start | bytes 15728640 | tf_op jit(solution)/shard_map/all_gather | solution.py:69
  7.3 440.7 %all-gather.4.cloned.1.call-start = ((), (), s32[]{:S(2)}) async-start(), calls=%async_computation.2 | async-start | bytes 15728640 | tf_op jit(solution)/shard_map/all_gather | solution.py:63
  8.0 24.9 %copy-start.6 = (f32[1536]{0:T(1024)S(1)}, f32[1536]{0:T(1024)}, u32[]{:S(2)}) copy-start(f32[1536]{0:T(1024)} %param.15) | copy-start | bytes 18436
  8.1 658.0 %all-gather.8.cloned.1.call-start = ((), (), s32[]{:S(2)}) async-start(), calls=%async_computation.4 | async-start | bytes 15728640 | tf_op jit(solution)/shard_map/all_gather | solution.py:76
  32.0 0.9 copy-start.2
  700.3 4.9 copy-start.8
  700.3 5.0 copy-start.4
  700.3 76.5 %all-to-all-start.1 = ((bf16[8,256,1536]{2,0,1:T(8,128)(2,1)}), bf16[8,256,1536]{2,0,1:T(8,128)(2,1)}, u32[]{:S(2)}, u32[]{:S(2)}) async-start(bf16[8,256,1536]{2,0,1:T(8,128)(2,1)} %copy.55), calls=%async_computation.1 | async-start | bytes 12582912 | tf_op jit(solution)/shard_map/all_to_all | solution.py:79
  784.2 23.7 %copy-start.1 = (bf16[128,1536]{1,0:T(8,128)(2,1)S(1)}, bf16[128,1536]{1,0:T(8,128)(2,1)}, u32[]{:S(2)}) copy-start(bf16[128,1536]{1,0:T(8,128)(2,1)} %param.12) | copy-start | bytes 1179652
  802.0 5.1 copy-start.7
Sparse Core Ops, SparseCore 0:
  9.0 220.9 all-gather.5
  231.5 216.4 all-gather.3
  449.6 216.3 all-gather.7
where the time goes:
time: 824 us; the launch traced here: 815 us
  waiting for transfers between devices  589 us (71%)
  blocking collectives  76.6 us (9%)
  local copies, waits for them, and re-layouts  63.5 us (8%)
  matrix products  41.8 us (5%)
  other arithmetic  24.8 us (3%)
  between operations  13.6 us (2%)
    all_gather x1, waiting for transfers between devices, body(): lax.all_gather(w_down, 'blk', axis=1, tiled=True)  218 us
    all_gather x1, waiting for transfers between devices, body(): lax.all_gather(w_gate, 'blk', axis=1, tiled=True)  205 us
    all_gather x1, waiting for transfers between devices, body(): lax.all_gather(w_up, 'blk', axis=1, tiled=True)  94 us
    all_to_all x1, blocking collectives, body(): lax.all_to_all(outgoing, 'tok', split_axis=1, concat_axis=1, tiled=True)  76.6 us
    all_to_all x1, waiting for transfers between devices, body(): lax.all_to_all(expert_y, 'tok', split_axis=1, concat_axis=1, tiled=True)  70.1 us
    dot_general x1, matrix products, body(): jnp.einsum('snf,sdf->snd', act, lax.all_gather(w_down, 'blk', axis=1, til...  25.3 us
    unnamed x26, local copies, waits for them, and re-layouts  21.1 us
    another operation x3, other arithmetic  18.2 us
  transfers between devices with their start and end apart: 4, of which 4 were waited for; matrix products, arithmetic and copies ran while one was open for 8% of the time, Pallas kernels for 0%

commit v1 on v0

--- a/solution.py
+++ b/solution.py
@@ -1,6 +1,10 @@
+import functools
+
 import jax
 import jax.numpy as jnp
 from jax import lax
+from jax.experimental import pallas as pl
+from jax.experimental.pallas import tpu as pltpu
 from jax.sharding import PartitionSpec as P
 
 eps = 1e-05
@@ -84,6 +88,317 @@
     return rms_scale(mixed, norm2_gain).astype(jnp.bfloat16)
 
 
+def flip(value, step):
+    return value + step * (1 - 2 * ((value // step) % 2))
+
+
+def turned(value, r):
+    value = flip(value, 1) if r & 1 else value
+    return flip(value, 2) if r & 2 else value
+
+
+def expert_kernel(
+    first_width,
+    sent_ref,
+    wg_ref,
+    wu_ref,
+    wd_ref,
+    out_ref,
+    tokens,
+    gates,
+    ups,
+    downs,
+    acts,
+    sums,
+    from_core,
+    from_far,
+    from_near,
+    from_blk,
+    send_sem,
+    recv_sem,
+    own_sem,
+):
+    a, b = lax.axis_index("tok"), lax.axis_index("blk")
+    a_core, a_x, a_y = flip(a, 1), flip(a, 2), flip(a, 4)
+    core, mx, my = a % 2, (a // 2) % 2, a // 4
+    far = flip(a_x, 4)
+    rows = sent_ref.shape[0]
+    half = rows // 2
+    sub = gates.shape[0]
+    block = downs.shape[2]
+    ff = gates.shape[2]
+    number = iter(range(send_sem.shape[0]))
+    started = []
+
+    def send(src, dst, device):
+        k = next(number)
+        copy = pltpu.make_async_remote_copy(
+            src_ref=src,
+            dst_ref=dst,
+            send_sem=send_sem.at[k],
+            recv_sem=recv_sem.at[k],
+            device_id=device,
+            device_id_type=pl.DeviceIdType.MESH,
+        )
+        copy.start()
+        started.append(copy)
+        return copy
+
+    barrier = pltpu.get_barrier_semaphore()
+    partners = [(a_core, b), (a_x, b), (a_y, b)] + [(a, turned(b, r)) for r in (1, 2, 3)]
+    for partner in partners:
+        pl.semaphore_signal(
+            barrier, inc=1, device_id=partner, device_id_type=pl.DeviceIdType.MESH
+        )
+    pl.semaphore_wait(barrier, len(partners))
+
+    own = a * 4 + b
+    tokens[own] = sent_ref[...]
+    by_blk = {r: send(tokens.at[own], tokens.at[own], (a, turned(b, r))) for r in (1, 2, 3)}
+    here = pl.ds(pl.multiple_of(b * block, 128), block)
+    mine = [
+        pltpu.make_async_copy(wg_ref.at[pl.ds(b * sub, sub)], gates.at[:, here], own_sem.at[0]),
+        pltpu.make_async_copy(wu_ref.at[pl.ds(b * sub, sub)], ups.at[:, here], own_sem.at[1]),
+        pltpu.make_async_copy(wd_ref.at[pl.ds(b * sub, sub)], downs.at[b], own_sem.at[2]),
+    ]
+    for copy in mine:
+        copy.start()
+    weights = []
+    for r in (3, 2, 1):
+        to = turned(b, r)
+        part = pl.ds(to * sub, sub)
+        weights.append(send(wg_ref.at[part], gates.at[:, here], (a, to)))
+        weights.append(send(wu_ref.at[part], ups.at[:, here], (a, to)))
+
+    def block_at(group, r):
+        return tokens.at[group * 4 + turned(b, r)]
+
+    def pass_on(group, r, to):
+        return send(block_at(group, r), block_at(group, r), (to, b))
+
+    by_x, by_y, by_core = {}, {}, []
+    for r in range(4):
+        if r:
+            by_blk[r].wait_recv()
+        by_x[r] = pass_on(a, r, a_x)
+        by_y[r] = pass_on(a, r, a_y)
+        by_core.append(pass_on(a, r, a_core))
+    far_y, far_x = {}, {}
+    for r in range(4):
+        by_x[r].wait_recv()
+        piece = tokens.at[a_x * 4 + turned(b, r), pl.ds(0, half)]
+        far_y[r] = send(piece, piece, (a_y, b))
+        by_core.append(pass_on(a_x, r, a_core))
+        by_y[r].wait_recv()
+        piece = tokens.at[a_y * 4 + turned(b, r), pl.ds(half, half)]
+        far_x[r] = send(piece, piece, (a_x, b))
+        by_core.append(pass_on(a_y, r, a_core))
+    for r in range(4):
+        far_y[r].wait_recv()
+        far_x[r].wait_recv()
+        by_core.append(pass_on(far, r, a_core))
+    for copy in by_core:
+        copy.wait_recv()
+
+    for copy in weights:
+        copy.wait_recv()
+    for copy in mine:
+        copy.wait()
+    later = {}
+    for r in (1, 3, 2):
+        to = turned(b, r)
+        later[r] = send(wd_ref.at[pl.ds(to * sub, sub)], downs.at[b], (a, to))
+
+    width = gates.shape[1]
+    tile = 4 * rows
+    first = first_width * a + sub * b
+    lanes = tokens.shape[2] - width
+    lane = lax.broadcasted_iota(jnp.int32, (tile, lanes), 1)
+
+    def expert_rows(t, carry):
+        x = tokens[pl.ds(t * 4, 4)].reshape(tile, tokens.shape[2])
+        parts = x[:, width:].astype(jnp.float32)
+        x = x[:, :width]
+        for s in range(sub):
+            at = (lane == first + s) | (lane == first + s + lanes // 2)
+            scale = jnp.sum(jnp.where(at, parts, 0.0), axis=1, keepdims=True)
+            gate = jnp.dot(x, gates[s], preferred_element_type=jnp.float32)
+            up = jnp.dot(x, ups[s], preferred_element_type=jnp.float32)
+            act = gate / (1.0 + jnp.exp(-gate)) * up * scale
+            acts[t, :, s * ff : (s + 1) * ff] = act.astype(jnp.bfloat16)
+        return carry
+
+    lax.fori_loop(0, 8, expert_rows, 0)
+
+    def weighted(r):
+        column = turned(b, r)
+
+        def down_rows(t, carry):
+            y = jnp.zeros((tile, block), jnp.float32)
+            for s in range(sub):
+                y = y + lax.dot_general(
+                    acts[t, :, s * ff : (s + 1) * ff],
+                    downs[column, s],
+                    (((1,), (1,)), ((), ())),
+                    preferred_element_type=jnp.float32,
+                )
+            sums[r, t % 2, t // 4, (t // 2) % 2] = y.astype(jnp.bfloat16)
+            return carry
+
+        if r:
+            later[r].wait_recv()
+        lax.fori_loop(0, 8, down_rows, 0)
+
+    def add(r, i, j, got):
+        sums[r, core, i, j] = (
+            sums[r, core, i, j].astype(jnp.float32) + got.astype(jnp.float32)
+        ).astype(jnp.bfloat16)
+
+    step = [{}, {}, {}, {}]
+
+    def send_core(r):
+        step[0][r] = send(sums.at[r, 1 - core], from_core.at[r], (a_core, b))
+
+    def send_far(r):
+        step[0][r].wait_recv()
+        for i in range(2):
+            for j in range(2):
+                add(r, i, j, from_core[r, i, j])
+        if r % 2 == 0:
+            step[1][r] = send(sums.at[r, core, :, 1 - mx], from_far.at[r], (a_x, b))
+        else:
+            step[1][r] = send(sums.at[r, core, 1 - my], from_far.at[r], (a_y, b))
+
+    def send_near(r):
+        step[1][r].wait_recv()
+        for i in range(2):
+            if r % 2 == 0:
+                add(r, i, mx, from_far[r, i])
+            else:
+                add(r, my, i, from_far[r, i])
+        if r % 2 == 0:
+            step[2][r] = send(sums.at[r, core, 1 - my, mx], from_near.at[r], (a_y, b))
+        else:
+            step[2][r] = send(sums.at[r, core, my, 1 - mx], from_near.at[r], (a_x, b))
+
+    def send_blk(r):
+        step[2][r].wait_recv()
+        add(r, my, mx, from_near[r])
+        columns = pl.ds(pl.multiple_of(turned(b, r) * block, 128), block)
+        for q in (3, 2, 1):
+            to = turned(b, q)
+            piece = pl.ds(pl.multiple_of(to * rows, 16), rows)
+            step[3][r, q] = send(
+                sums.at[r, core, my, mx, piece], from_blk.at[q - 1, :, columns], (a, to)
+            )
+        kept = sums[r, core, my, mx, pl.ds(pl.multiple_of(b * rows, 16), rows)]
+        out_ref[:, columns] = kept.astype(jnp.float32)
+
+    for r, n in ((0, 0), (1, 1), (3, 2), (2, 3)):
+        weighted(r)
+        send_core(r)
+        if n >= 1:
+            send_far((0, 1, 3)[n - 1])
+    send_near(0)
+    send_far(2)
+    send_near(1)
+    send_blk(0)
+    send_near(3)
+    send_blk(1)
+    send_near(2)
+    send_blk(3)
+    send_blk(2)
+    for copy in step[3].values():
+        copy.wait_recv()
+    out_ref[...] += (
+        from_blk[0].astype(jnp.float32)
+        + from_blk[1].astype(jnp.float32)
+        + from_blk[2].astype(jnp.float32)
+    )
+    for copy in started:
+        copy.wait_send()
+
+
+def expert_sum(sent, w_gate, w_up, w_down):
+    rows, sent_width = sent.shape
+    slot_dev, block, ff = w_gate.shape
+    sub = slot_dev // 4
+    width = 4 * block
+    tile = 4 * rows
+    copies = 3 + 6 + 12 + 16 + 4 + 3 + 12 + 12
+    bf16 = jnp.bfloat16
+    macs = 32 * rows * sub * ff * width * 3
+    return pl.pallas_call(
+        functools.partial(expert_kernel, slot_dev),
+        out_shape=jax.ShapeDtypeStruct((rows, width), jnp.float32),
+        in_specs=[pl.BlockSpec(memory_space=pltpu.VMEM)]
+        + [pl.BlockSpec(memory_space=pl.ANY)] * 3,
+        out_specs=pl.BlockSpec(memory_space=pltpu.VMEM),
+        scratch_shapes=[
+            pltpu.VMEM((32, rows, sent_width), bf16),
+            pltpu.VMEM((sub, width, ff), bf16),
+            pltpu.VMEM((sub, width, ff), bf16),
+            pltpu.VMEM((4, sub, block, ff), bf16),
+            pltpu.VMEM((8, tile, sub * ff), bf16),
+            pltpu.VMEM((4, 2, 2, 2, tile, block), bf16),
+            pltpu.VMEM((4, 2, 2, tile, block), bf16),
+            pltpu.VMEM((4, 2, tile, block), bf16),
+            pltpu.VMEM((4, tile, block), bf16),
+            pltpu.VMEM((3, rows, width), bf16),
+            pltpu.SemaphoreType.DMA((copies,)),
+            pltpu.SemaphoreType.DMA((copies,)),
+            pltpu.SemaphoreType.DMA((3,)),
+        ],
+        compiler_params=pltpu.CompilerParams(
+            collective_id=0, has_side_effects=True, vmem_limit_bytes=63 * 1024 * 1024
+        ),
+        cost_estimate=pl.CostEstimate(
+            flops=2 * macs, bytes_accessed=3 * slot_dev * block * ff * 2, transcendentals=0
+        ),
+    )(sent, w_gate, w_up, w_down)
+
+
+def whole_slot_plan(
+    attn_out,
+    resid,
+    w_o,
+    norm1_gain,
+    router_w,
+    route_slot,
+    slot_expert,
+    keep,
+    w_gate,
+    w_up,
+    w_down,
+    norm2_gain,
+):
+    rows = route_slot.shape[0]
+    slots = w_gate.shape[0] * lax.axis_size("tok")
+
+    hidden_state = resid.astype(jnp.float32) + jnp.dot(
+        attn_out, w_o, preferred_element_type=jnp.float32
+    )
+    normed = rms_scale(hidden_state, norm1_gain).astype(jnp.bfloat16)
+    expert_pick = slot_expert[None, :] == jnp.arange(router_w.shape[1], dtype=jnp.int32)[:, None]
+    logits = jnp.dot(normed.astype(jnp.float32), router_w, precision=lax.Precision.HIGHEST)
+    slot_logits = jnp.sum(jnp.where(expert_pick[None], logits[:, :, None], 0.0), axis=1)
+    hits = jnp.any(
+        route_slot[:, :, None] == jnp.arange(slots, dtype=jnp.int32)[None, None, :], axis=1
+    )
+    top_logit = jnp.max(jnp.where(hits, slot_logits, -jnp.inf), axis=1, keepdims=True)
+    powers = jnp.where(hits, jnp.exp(jnp.where(hits, slot_logits, top_logit) - top_logit), 0.0)
+    probs = powers / jnp.sum(powers, axis=1, keepdims=True)
+    probs = jnp.where((keep > 0)[:, None], probs, 0.0)
+    high = lax.reduce_precision(probs, 8, 7)
+    low = probs - high
+    sent = jnp.concatenate(
+        [normed, high.astype(jnp.bfloat16), low.astype(jnp.bfloat16)], axis=1
+    )
+    moe = expert_sum(sent, w_gate, w_up, w_down)
+    mixed = hidden_state + moe
+    return rms_scale(mixed, norm2_gain).astype(jnp.bfloat16)
+
+
 def solution(mesh):
     placed = (
         P(("tok", "blk"), None),
@@ -99,6 +414,18 @@
         P("tok", "blk", None),
         P(),
     )
-    return jax.shard_map(
-        body, mesh=mesh, in_specs=placed, out_specs=P(("tok", "blk"), None), check_vma=False
-    )
+    groups, blocks = mesh.shape["tok"], mesh.shape["blk"]
+
+    def layer(*args):
+        slot_dev = args[8].shape[0] // groups
+        cube = groups == 8 and blocks == 4 and slot_dev % blocks == 0
+        plan = whole_slot_plan if cube else body
+        return jax.shard_map(
+            plan,
+            mesh=mesh,
+            in_specs=placed,
+            out_specs=P(("tok", "blk"), None),
+            check_vma=False,
+        )(*args)
+
+    return layer

time: 824 us -> 318 us (0.39); the launches traced: 815 us -> 318 us
  waiting for transfers between devices: 589 us -> 0 us
  Pallas kernels: 0 us -> 306 us
  blocking collectives: 76.6 us -> 0 us
  local copies, waits for them, and re-layouts: 63.5 us -> 1.95 us
  matrix products: 41.8 us -> 3.82 us
  other arithmetic: 24.8 us -> 5.61 us
  between operations: 13.6 us -> 0.12 us
    all_gather x3 -> x0, waiting for transfers between devices: 517 us -> none  [the longest x1 218 us: body(): lax.all_gather(w_down, 'blk', axis=1, tiled=True)]
    pallas_call x0 -> x1, Pallas kernels: none -> 306 us  [expert_sum(): pl.pallas_call(functools.partial(expert_kernel, slot_dev), out_shape=jax....]
    all_to_all x1 -> x0, blocking collectives: 76.6 us -> none  [body(): lax.all_to_all(outgoing, 'tok', split_axis=1, concat_axis=1, tiled=True)]
    all_to_all x1 -> x0, waiting for transfers between devices: 70.1 us -> none  [body(): lax.all_to_all(expert_y, 'tok', split_axis=1, concat_axis=1, tiled=True)]
    dot_general x4 -> x2, matrix products: 41.8 us -> 3.82 us  [the longest x1 3.33 us: whole_slot_plan(): jnp.dot(attn_out, w_o, preferred_element_type=jnp.float32)]
    unnamed x26 -> x10, local copies, waits for them, and re-layouts: 21.1 us -> 0.88 us
    another operation x3 -> x0, other arithmetic: 18.2 us -> none
    gather x1 -> x0, local copies, waits for them, and re-layouts: 17.8 us -> none  [body(): picked = returned[local, target_row]]
  transfers between devices with their start and end apart: 4 -> 0, of which waited for: 4 -> 0; matrix products, arithmetic and copies ran while one was open for 8% -> 0% of each run, Pallas kernels for 0% -> 0%
where the time goes in v1:
time: 318 us
  Pallas kernels  306 us (96%)
  other arithmetic  5.61 us (2%)
  matrix products  3.82 us (1%)
    pallas_call x1, Pallas kernels, expert_sum(): pl.pallas_call(functools.partial(expert_kernel, slot_dev), out_shape=jax....  306 us

profile of v1, /device:TPU:0, one launch (start us, length us, event | category | flops | bytes accessed | tf_op | source)
XLA Modules:
  0.0 317.7 jit_solution(9059321312858631746)
XLA Ops:
  0.0 0.0 copy-start
  0.0 0.7 broadcast_compare_fusion
  0.7 0.7 iota_compare_fusion.1
  1.4 0.7 fusion
  2.1 0.1 copy.17
  2.2 0.0 copy-done
  2.2 0.0 copy-start.3
  2.2 0.0 copy-start.2
  2.3 3.3 %multiply_reduce_fusion.1 = (f32[128]{0:T(128)S(1)}, f32[128,1536]{1,0:T(8,128)S(1)}) fusion(bf16[128,1536]{1,0:T(8,128)(2,1)S(1)} %copy-done, bf16[1536,1536]{1,0:T(8,128)(2,1)} %param.14, bf16[128,1536]{1,0:T(8,128)(2,1)} %param.13), kind=kOutput, calls=%fused_computation.5 | convolution fusion | flops 604766080 | bytes 6291968 | tf_op jit(solution)/shard_map/dot_general | solution.py:378
  5.6 0.0 copy-start.1
  5.6 0.9 copy-done.1
  6.5 0.0 copy-done.3
  6.5 0.1 multiply_convert_fusion.1
  6.6 0.0 copy-done.2
  6.6 0.5 fusion.3
  7.1 0.6 select_reduce_fusion
  7.8 0.1 copy.16
  7.9 0.2 fusion.2
  8.0 0.1 fusion.1
  8.2 0.9 concatenate.3.sent_ref
  9.1 0.0 copy-start.4
  9.1 306.2 %shard_map.118 = f32[128,1536]{1,0:T(8,128)} custom-call(bf16[128,1664]{1,0:T(8,128)(2,1)} %concatenate.3.sent_ref, bf16[8,384,512]{2,1,0:T(8,128)(2,1)} %wg_ref.1, bf16[8,384,512]{2,1,0:T(8,128)(2,1)} %wu_ref.1, bf16[8,384,512]{2,1,0:T(8,128)(2,1)} %wd_ref.1), custom_call_target="tpu_custom_call" | custom-call | flops 38654705664 | bytes 9437184 | tf_op jit(solution)/shard_map/pallas_call | solution.py:331
  315.3 1.5 multiply_reduce_fusion
  316.9 0.0 copy-done.4
  316.9 0.9 multiply_convert_fusion
  (4 shorter events, 0.0 us)
Async XLA Ops:
  0.0 2.2 copy-start
  2.2 4.2 %copy-start.3 = (f32[1536]{0:T(1024)S(1)}, f32[1536]{0:T(1024)}, u32[]{:S(2)}) copy-start(f32[1536]{0:T(1024)} %param.15) | copy-start | bytes 18436
  2.2 4.4 %copy-start.2 = (f32[1536,40]{0,1:T(8,128)S(1)}, f32[1536,40]{0,1:T(8,128)}, u32[]{:S(2)}) copy-start(f32[1536,40]{0,1:T(8,128)} %param.16) | copy-start | bytes 737284
  5.6 0.9 copy-start.1
  9.1 307.8 %copy-start.4 = (f32[1536]{0:T(1024)S(1)}, f32[1536]{0:T(1024)}, u32[]{:S(2)}) copy-start(f32[1536]{0:T(1024)} %param.23) | copy-start | bytes 18436

commit v2 on v1

--- a/solution.py
+++ b/solution.py
@@ -1,5 +1,3 @@
-import functools
-
 import jax
 import jax.numpy as jnp
 from jax import lax
@@ -98,12 +96,20 @@
 
 
 def expert_kernel(
-    first_width,
-    sent_ref,
+    attn_ref,
+    resid_ref,
+    gain1_ref,
+    router_ref,
+    route_ref,
+    expert_ref,
+    keep_ref,
+    gain2_ref,
+    wo_ref,
     wg_ref,
     wu_ref,
     wd_ref,
     out_ref,
+    hidden,
     tokens,
     gates,
     ups,
@@ -122,11 +128,12 @@
     a_core, a_x, a_y = flip(a, 1), flip(a, 2), flip(a, 4)
     core, mx, my = a % 2, (a // 2) % 2, a // 4
     far = flip(a_x, 4)
-    rows = sent_ref.shape[0]
+    rows = attn_ref.shape[0]
+    tile = 4 * rows
     half = rows // 2
     sub = gates.shape[0]
     block = downs.shape[2]
-    ff = gates.shape[2]
+    width, ff = gates.shape[1:]
     number = iter(range(send_sem.shape[0]))
     started = []
 
@@ -153,9 +160,30 @@
     pl.semaphore_wait(barrier, len(partners))
 
     own = a * 4 + b
-    tokens[own] = sent_ref[...]
-    by_blk = {r: send(tokens.at[own], tokens.at[own], (a, turned(b, r))) for r in (1, 2, 3)}
     here = pl.ds(pl.multiple_of(b * block, 128), block)
+    weights = {}
+
+    def send_slot(s):
+        weights[s] = []
+        for r in (3, 2, 1):
+            to = turned(b, r)
+            weights[s].append(send(wg_ref.at[to * sub + s], gates.at[s, here], (a, to)))
+            weights[s].append(send(wu_ref.at[to * sub + s], ups.at[s, here], (a, to)))
+
+    projection = []
+    for k in range(3):
+        part = pl.ds(k * tile, tile)
+        projection.append((wo_ref.at[part, pl.ds(0, 2 * tile)], acts.at[k]))
+        projection.append(
+            (wo_ref.at[part, pl.ds(2 * tile, tile)], acts.at[3 + k, :, pl.ds(0, tile)])
+        )
+    projection = [
+        pltpu.make_async_copy(src, dst, own_sem.at[3 + k])
+        for k, (src, dst) in enumerate(projection)
+    ]
+    for copy in projection:
+        copy.start()
+    send_slot(0)
     mine = [
         pltpu.make_async_copy(wg_ref.at[pl.ds(b * sub, sub)], gates.at[:, here], own_sem.at[0]),
         pltpu.make_async_copy(wu_ref.at[pl.ds(b * sub, sub)], ups.at[:, here], own_sem.at[1]),
@@ -163,12 +191,44 @@
     ]
     for copy in mine:
         copy.start()
-    weights = []
-    for r in (3, 2, 1):
-        to = turned(b, r)
-        part = pl.ds(to * sub, sub)
-        weights.append(send(wg_ref.at[part], gates.at[:, here], (a, to)))
-        weights.append(send(wu_ref.at[part], ups.at[:, here], (a, to)))
+    for copy in projection:
+        copy.wait()
+    for k in range(3):
+        x = attn_ref[:, k * tile : (k + 1) * tile]
+        left = jnp.dot(x, acts[k], preferred_element_type=jnp.float32)
+        right = jnp.dot(x, acts[3 + k, :, :tile], preferred_element_type=jnp.float32)
+        if k == 0:
+            hidden[:, : 2 * tile] = left
+            hidden[:, 2 * tile :] = right
+        else:
+            hidden[:, : 2 * tile] += left
+            hidden[:, 2 * tile :] += right
+    hidden[...] += resid_ref[...].astype(jnp.float32)
+    normed = rms_scale(hidden[...], gain1_ref[...]).astype(jnp.bfloat16)
+    logits = jnp.dot(
+        normed.astype(jnp.float32),
+        router_ref[...],
+        precision=lax.Precision.HIGHEST,
+        preferred_element_type=jnp.float32,
+    )
+    slots = expert_ref.shape[1]
+    slot_logits = jnp.zeros((rows, slots), jnp.float32)
+    for e in range(router_ref.shape[1]):
+        slot_logits = jnp.where(expert_ref[...] == e, logits[:, e : e + 1], slot_logits)
+    slot_of = lax.broadcasted_iota(jnp.int32, (rows, slots), 1)
+    hits = slot_of == route_ref[:, 0:1]
+    for k in range(1, route_ref.shape[1]):
+        hits = hits | (slot_of == route_ref[:, k : k + 1])
+    top_logit = jnp.max(jnp.where(hits, slot_logits, -jnp.inf), axis=1, keepdims=True)
+    powers = jnp.exp(jnp.where(hits, slot_logits, top_logit) - top_logit)
+    powers = jnp.where(hits, powers, 0.0)
+    probs = powers / jnp.sum(powers, axis=1, keepdims=True)
+    probs = jnp.where(keep_ref[...] > 0, probs, 0.0)
+    high = probs.astype(jnp.bfloat16)
+    low = (probs - high.astype(jnp.float32)).astype(jnp.bfloat16)
+    tokens[own, :, :width] = normed
+    tokens[own, :, width:] = jnp.concatenate([high, low], axis=1)
+    by_blk = {r: send(tokens.at[own], tokens.at[own], (a, turned(b, r))) for r in (2, 1)}
 
     def block_at(group, r):
         return tokens.at[group * 4 + turned(b, r)]
@@ -177,14 +237,16 @@
         return send(block_at(group, r), block_at(group, r), (to, b))
 
     by_x, by_y, by_core = {}, {}, []
-    for r in range(4):
+    for r in (0, 2, 1, 3):
         if r:
             by_blk[r].wait_recv()
+        if r == 2:
+            by_blk[3] = send(block_at(a, 2), block_at(a, 2), (a, turned(b, 1)))
         by_x[r] = pass_on(a, r, a_x)
         by_y[r] = pass_on(a, r, a_y)
         by_core.append(pass_on(a, r, a_core))
     far_y, far_x = {}, {}
-    for r in range(4):
+    for r in (0, 2, 1, 3):
         by_x[r].wait_recv()
         piece = tokens.at[a_x * 4 + turned(b, r), pl.ds(0, half)]
         far_y[r] = send(piece, piece, (a_y, b))
@@ -193,42 +255,48 @@
         piece = tokens.at[a_y * 4 + turned(b, r), pl.ds(half, half)]
         far_x[r] = send(piece, piece, (a_x, b))
         by_core.append(pass_on(a_y, r, a_core))
-    for r in range(4):
+    for s in range(1, sub):
+        send_slot(s)
+    for r in (0, 2, 1, 3):
         far_y[r].wait_recv()
         far_x[r].wait_recv()
         by_core.append(pass_on(far, r, a_core))
     for copy in by_core:
         copy.wait_recv()
 
-    for copy in weights:
-        copy.wait_recv()
     for copy in mine:
         copy.wait()
     later = {}
-    for r in (1, 3, 2):
+
+    def send_down(r):
         to = turned(b, r)
         later[r] = send(wd_ref.at[pl.ds(to * sub, sub)], downs.at[b], (a, to))
 
-    width = gates.shape[1]
-    tile = 4 * rows
-    first = first_width * a + sub * b
+    first = sub * own
     lanes = tokens.shape[2] - width
     lane = lax.broadcasted_iota(jnp.int32, (tile, lanes), 1)
 
-    def expert_rows(t, carry):
-        x = tokens[pl.ds(t * 4, 4)].reshape(tile, tokens.shape[2])
-        parts = x[:, width:].astype(jnp.float32)
-        x = x[:, :width]
-        for s in range(sub):
+    for s in range(sub):
+
+        def expert_rows(t, carry):
+            x = tokens[pl.ds(t * 4, 4)].reshape(tile, tokens.shape[2])
+            parts = x[:, width:].astype(jnp.float32)
+            x = x[:, :width]
             at = (lane == first + s) | (lane == first + s + lanes // 2)
             scale = jnp.sum(jnp.where(at, parts, 0.0), axis=1, keepdims=True)
             gate = jnp.dot(x, gates[s], preferred_element_type=jnp.float32)
             up = jnp.dot(x, ups[s], preferred_element_type=jnp.float32)
             act = gate / (1.0 + jnp.exp(-gate)) * up * scale
             acts[t, :, s * ff : (s + 1) * ff] = act.astype(jnp.bfloat16)
-        return carry
-
-    lax.fori_loop(0, 8, expert_rows, 0)
+            return carry
+
+        for copy in weights[s]:
+            copy.wait_recv()
+        if s == sub - 1:
+            send_down(1)
+            send_down(3)
+        lax.fori_loop(0, 8, expert_rows, 0)
+    send_down(2)
 
     def weighted(r):
         column = turned(b, r)
@@ -292,7 +360,7 @@
                 sums.at[r, core, my, mx, piece], from_blk.at[q - 1, :, columns], (a, to)
             )
         kept = sums[r, core, my, mx, pl.ds(pl.multiple_of(b * rows, 16), rows)]
-        out_ref[:, columns] = kept.astype(jnp.float32)
+        hidden[:, columns] += kept.astype(jnp.float32)
 
     for r, n in ((0, 0), (1, 1), (3, 2), (2, 3)):
         weighted(r)
@@ -310,52 +378,14 @@
     send_blk(2)
     for copy in step[3].values():
         copy.wait_recv()
-    out_ref[...] += (
+    mixed = hidden[...] + (
         from_blk[0].astype(jnp.float32)
         + from_blk[1].astype(jnp.float32)
         + from_blk[2].astype(jnp.float32)
     )
+    out_ref[...] = rms_scale(mixed, gain2_ref[...]).astype(jnp.bfloat16)
     for copy in started:
         copy.wait_send()
-
-
-def expert_sum(sent, w_gate, w_up, w_down):
-    rows, sent_width = sent.shape
-    slot_dev, block, ff = w_gate.shape
-    sub = slot_dev // 4
-    width = 4 * block
-    tile = 4 * rows
-    copies = 3 + 6 + 12 + 16 + 4 + 3 + 12 + 12
-    bf16 = jnp.bfloat16
-    macs = 32 * rows * sub * ff * width * 3
-    return pl.pallas_call(
-        functools.partial(expert_kernel, slot_dev),
-        out_shape=jax.ShapeDtypeStruct((rows, width), jnp.float32),
-        in_specs=[pl.BlockSpec(memory_space=pltpu.VMEM)]
-        + [pl.BlockSpec(memory_space=pl.ANY)] * 3,
-        out_specs=pl.BlockSpec(memory_space=pltpu.VMEM),
-        scratch_shapes=[
-            pltpu.VMEM((32, rows, sent_width), bf16),
-            pltpu.VMEM((sub, width, ff), bf16),
-            pltpu.VMEM((sub, width, ff), bf16),
-            pltpu.VMEM((4, sub, block, ff), bf16),
-            pltpu.VMEM((8, tile, sub * ff), bf16),
-            pltpu.VMEM((4, 2, 2, 2, tile, block), bf16),
-            pltpu.VMEM((4, 2, 2, tile, block), bf16),
-            pltpu.VMEM((4, 2, tile, block), bf16),
-            pltpu.VMEM((4, tile, block), bf16),
-            pltpu.VMEM((3, rows, width), bf16),
-            pltpu.SemaphoreType.DMA((copies,)),
-            pltpu.SemaphoreType.DMA((copies,)),
-            pltpu.SemaphoreType.DMA((3,)),
-        ],
-        compiler_params=pltpu.CompilerParams(
-            collective_id=0, has_side_effects=True, vmem_limit_bytes=63 * 1024 * 1024
-        ),
-        cost_estimate=pl.CostEstimate(
-            flops=2 * macs, bytes_accessed=3 * slot_dev * block * ff * 2, transcendentals=0
-        ),
-    )(sent, w_gate, w_up, w_down)
 
 
 def whole_slot_plan(
@@ -372,31 +402,56 @@
     w_down,
     norm2_gain,
 ):
-    rows = route_slot.shape[0]
-    slots = w_gate.shape[0] * lax.axis_size("tok")
-
-    hidden_state = resid.astype(jnp.float32) + jnp.dot(
-        attn_out, w_o, preferred_element_type=jnp.float32
-    )
-    normed = rms_scale(hidden_state, norm1_gain).astype(jnp.bfloat16)
-    expert_pick = slot_expert[None, :] == jnp.arange(router_w.shape[1], dtype=jnp.int32)[:, None]
-    logits = jnp.dot(normed.astype(jnp.float32), router_w, precision=lax.Precision.HIGHEST)
-    slot_logits = jnp.sum(jnp.where(expert_pick[None], logits[:, :, None], 0.0), axis=1)
-    hits = jnp.any(
-        route_slot[:, :, None] == jnp.arange(slots, dtype=jnp.int32)[None, None, :], axis=1
-    )
-    top_logit = jnp.max(jnp.where(hits, slot_logits, -jnp.inf), axis=1, keepdims=True)
-    powers = jnp.where(hits, jnp.exp(jnp.where(hits, slot_logits, top_logit) - top_logit), 0.0)
-    probs = powers / jnp.sum(powers, axis=1, keepdims=True)
-    probs = jnp.where((keep > 0)[:, None], probs, 0.0)
-    high = lax.reduce_precision(probs, 8, 7)
-    low = probs - high
-    sent = jnp.concatenate(
-        [normed, high.astype(jnp.bfloat16), low.astype(jnp.bfloat16)], axis=1
-    )
-    moe = expert_sum(sent, w_gate, w_up, w_down)
-    mixed = hidden_state + moe
-    return rms_scale(mixed, norm2_gain).astype(jnp.bfloat16)
+    rows, width = resid.shape
+    slot_dev, block, ff = w_gate.shape
+    sub = slot_dev // 4
+    slots = slot_expert.shape[0]
+    tile = 4 * rows
+    copies = 3 + 6 * sub + 12 + 16 + 4 + 3 + 12 + 12
+    bf16 = jnp.bfloat16
+    macs = 32 * rows * sub * ff * width * 3
+    return pl.pallas_call(
+        expert_kernel,
+        out_shape=jax.ShapeDtypeStruct((rows, width), bf16),
+        in_specs=[pl.BlockSpec(memory_space=pltpu.VMEM)] * 8
+        + [pl.BlockSpec(memory_space=pl.ANY)] * 4,
+        out_specs=pl.BlockSpec(memory_space=pltpu.VMEM),
+        scratch_shapes=[
+            pltpu.VMEM((rows, width), jnp.float32),
+            pltpu.VMEM((32, rows, width + 2 * slots), bf16),
+            pltpu.VMEM((sub, width, ff), bf16),
+            pltpu.VMEM((sub, width, ff), bf16),
+            pltpu.VMEM((4, sub, block, ff), bf16),
+            pltpu.VMEM((8, tile, sub * ff), bf16),
+            pltpu.VMEM((4, 2, 2, 2, tile, block), bf16),
+            pltpu.VMEM((4, 2, 2, tile, block), bf16),
+            pltpu.VMEM((4, 2, tile, block), bf16),
+            pltpu.VMEM((4, tile, block), bf16),
+            pltpu.VMEM((3, rows, width), bf16),
+            pltpu.SemaphoreType.DMA((copies,)),
+            pltpu.SemaphoreType.DMA((copies,)),
+            pltpu.SemaphoreType.DMA((9,)),
+        ],
+        compiler_params=pltpu.CompilerParams(
+            collective_id=0, has_side_effects=True, vmem_limit_bytes=63 * 1024 * 1024
+        ),
+        cost_estimate=pl.CostEstimate(
+            flops=2 * macs, bytes_accessed=3 * slot_dev * block * ff * 2, transcendentals=0
+        ),
+    )(
+        attn_out,
+        resid,
+        norm1_gain.reshape(1, width),
+        router_w,
+        route_slot,
+        slot_expert.reshape(1, slots),
+        keep.reshape(rows, 1),
+        norm2_gain.reshape(1, width),
+        w_o,
+        w_gate,
+        w_up,
+        w_down,
+    )
 
 
 def solution(mesh):
@@ -418,7 +473,9 @@
 
     def layer(*args):
         slot_dev = args[8].shape[0] // groups
-        cube = groups == 8 and blocks == 4 and slot_dev % blocks == 0
+        rows, width = args[1].shape[0] // (groups * blocks), args[1].shape[1]
+        fits = slot_dev == 8 and args[8].shape[2] == 4 * rows and width == 12 * rows
+        cube = groups == 8 and blocks == 4 and fits and args[2].shape == (width, width)
         plan = whole_slot_plan if cube else body
         return jax.shard_map(
             plan,

time: 318 us -> 323 us (1.016)
  local copies, waits for them, and re-layouts: 1.95 us -> 9.24 us
  Pallas kernels: 306 us -> 313 us
  other arithmetic: 5.61 us -> 0 us
  matrix products: 3.82 us -> 0 us
    pallas_call x1, Pallas kernels: 306 us -> 313 us  [whole_slot_plan(): pl.pallas_call(expert_kernel, out_shape=jax.ShapeDtypeStruct((rows, width...]
    unnamed x10 -> x3, local copies, waits for them, and re-layouts: 0.88 us -> 5.27 us
    reshape x0 -> x3, local copies, waits for them, and re-layouts: none -> 3.96 us  [the longest x1 1.38 us: whole_slot_plan(): keep.reshape(rows, 1)]
    dot_general x2 -> x0, matrix products: 3.82 us -> none  [the longest x1 3.33 us: whole_slot_plan(): jnp.dot(attn_out, w_o, preferred_element_type=jnp.float32)]
where the time goes in v2:
time: 323 us
  Pallas kernels  313 us (97%)
  local copies, waits for them, and re-layouts  9.24 us (3%)
    pallas_call x1, Pallas kernels, whole_slot_plan(): pl.pallas_call(expert_kernel, out_shape=jax.ShapeDtypeStruct((rows, width...  313 us

profile of v2, /device:TPU:0, one launch (start us, length us, event | category | flops | bytes accessed | tf_op | source)
XLA Modules:
  0.0 322.6 jit_solution(1640890588443311589)
XLA Ops:
  0.0 1.3 reshape.12.gain1_ref
  1.3 1.3 reshape.15.gain2_ref
  2.6 1.4 copy.14.route_ref
  4.0 1.4 copy.15.keep_ref
  5.4 2.1 copy.13.router_ref
  7.5 313.4 %shard_map.118 = bf16[128,1536]{1,0:T(8,128)(2,1)} custom-call(bf16[128,1536]{1,0:T(8,128)(2,1)} %attn_ref.1, bf16[128,1536]{1,0:T(8,128)(2,1)} %resid_ref.1, f32[1,1536]{1,0:T(1,128)} %reshape.12.gain1_ref, f32[1536,40]{1,0:T(8,128)} %copy.13.router_ref, s32[128,8]{1,0:T(8,128)} %copy.14.route_ref, s32[1,64]{1,0:T(1,128)} %bitcast.3, ...), custom_call_target="tpu_custom_call" | custom-call | flops 38654705664 | bytes 9437184 | tf_op jit(solution)/shard_map/pallas_call | solution.py:413
  320.9 1.8 copy.17

commit v3 on v2

--- a/solution.py
+++ b/solution.py
@@ -99,11 +99,11 @@
     attn_ref,
     resid_ref,
     gain1_ref,
+    gain2_ref,
     router_ref,
     route_ref,
     expert_ref,
     keep_ref,
-    gain2_ref,
     wo_ref,
     wg_ref,
     wu_ref,
@@ -161,14 +161,19 @@
 
     own = a * 4 + b
     here = pl.ds(pl.multiple_of(b * block, 128), block)
-    weights = {}
-
-    def send_slot(s):
-        weights[s] = []
-        for r in (3, 2, 1):
+    weights = {s: [] for s in range(sub)}
+    waiting = [
+        (s, r, src, dst)
+        for s in range(sub)
+        for r in (3, 2, 1)
+        for src, dst in ((wg_ref, gates), (wu_ref, ups))
+    ]
+
+    def send_weight():
+        if waiting:
+            s, r, src, dst = waiting.pop(0)
             to = turned(b, r)
-            weights[s].append(send(wg_ref.at[to * sub + s], gates.at[s, here], (a, to)))
-            weights[s].append(send(wu_ref.at[to * sub + s], ups.at[s, here], (a, to)))
+            weights[s].append(send(src.at[to * sub + s], dst.at[s, here], (a, to)))
 
     projection = []
     for k in range(3):
@@ -183,7 +188,7 @@
     ]
     for copy in projection:
         copy.start()
-    send_slot(0)
+    send_weight()
     mine = [
         pltpu.make_async_copy(wg_ref.at[pl.ds(b * sub, sub)], gates.at[:, here], own_sem.at[0]),
         pltpu.make_async_copy(wu_ref.at[pl.ds(b * sub, sub)], ups.at[:, here], own_sem.at[1]),
@@ -204,26 +209,27 @@
             hidden[:, : 2 * tile] += left
             hidden[:, 2 * tile :] += right
     hidden[...] += resid_ref[...].astype(jnp.float32)
-    normed = rms_scale(hidden[...], gain1_ref[...]).astype(jnp.bfloat16)
-    logits = jnp.dot(
+    normed = rms_scale(hidden[...], gain1_ref[...].reshape(1, width)).astype(jnp.bfloat16)
+    logits = lax.dot_general(
         normed.astype(jnp.float32),
         router_ref[...],
+        (((1,), (1,)), ((), ())),
         precision=lax.Precision.HIGHEST,
         preferred_element_type=jnp.float32,
     )
     slots = expert_ref.shape[1]
     slot_logits = jnp.zeros((rows, slots), jnp.float32)
-    for e in range(router_ref.shape[1]):
+    for e in range(router_ref.shape[0]):
         slot_logits = jnp.where(expert_ref[...] == e, logits[:, e : e + 1], slot_logits)
     slot_of = lax.broadcasted_iota(jnp.int32, (rows, slots), 1)
-    hits = slot_of == route_ref[:, 0:1]
-    for k in range(1, route_ref.shape[1]):
-        hits = hits | (slot_of == route_ref[:, k : k + 1])
+    route = jnp.where(keep_ref[...] > 0, route_ref[...], -1).T
+    hits = slot_of == route[:, 0:1]
+    for k in range(1, route.shape[1]):
+        hits = hits | (slot_of == route[:, k : k + 1])
     top_logit = jnp.max(jnp.where(hits, slot_logits, -jnp.inf), axis=1, keepdims=True)
     powers = jnp.exp(jnp.where(hits, slot_logits, top_logit) - top_logit)
     powers = jnp.where(hits, powers, 0.0)
-    probs = powers / jnp.sum(powers, axis=1, keepdims=True)
-    probs = jnp.where(keep_ref[...] > 0, probs, 0.0)
+    probs = jnp.where(hits, powers / jnp.sum(powers, axis=1, keepdims=True), 0.0)
     high = probs.astype(jnp.bfloat16)
     low = (probs - high.astype(jnp.float32)).astype(jnp.bfloat16)
     tokens[own, :, :width] = normed
@@ -245,6 +251,7 @@
         by_x[r] = pass_on(a, r, a_x)
         by_y[r] = pass_on(a, r, a_y)
         by_core.append(pass_on(a, r, a_core))
+        send_weight()
     far_y, far_x = {}, {}
     for r in (0, 2, 1, 3):
         by_x[r].wait_recv()
@@ -255,12 +262,14 @@
         piece = tokens.at[a_y * 4 + turned(b, r), pl.ds(half, half)]
         far_x[r] = send(piece, piece, (a_x, b))
         by_core.append(pass_on(a_y, r, a_core))
-    for s in range(1, sub):
-        send_slot(s)
+        send_weight()
     for r in (0, 2, 1, 3):
         far_y[r].wait_recv()
         far_x[r].wait_recv()
         by_core.append(pass_on(far, r, a_core))
+        send_weight()
+    while waiting:
+        send_weight()
     for copy in by_core:
         copy.wait_recv()
 
@@ -292,11 +301,10 @@
 
         for copy in weights[s]:
             copy.wait_recv()
-        if s == sub - 1:
-            send_down(1)
-            send_down(3)
+        if s == 0:
+            for r in (1, 3, 2):
+                send_down(r)
         lax.fori_loop(0, 8, expert_rows, 0)
-    send_down(2)
 
     def weighted(r):
         column = turned(b, r)
@@ -383,7 +391,7 @@
         + from_blk[1].astype(jnp.float32)
         + from_blk[2].astype(jnp.float32)
     )
-    out_ref[...] = rms_scale(mixed, gain2_ref[...]).astype(jnp.bfloat16)
+    out_ref[...] = rms_scale(mixed, gain2_ref[...].reshape(1, width)).astype(jnp.bfloat16)
     for copy in started:
         copy.wait_send()
 
@@ -441,12 +449,12 @@
     )(
         attn_out,
         resid,
-        norm1_gain.reshape(1, width),
-        router_w,
-        route_slot,
+        norm1_gain,
+        norm2_gain,
+        router_w.T,
+        route_slot.T,
         slot_expert.reshape(1, slots),
-        keep.reshape(rows, 1),
-        norm2_gain.reshape(1, width),
+        keep.reshape(1, rows),
         w_o,
         w_gate,
         w_up,

time: 323 us -> 299 us (0.926)
  Pallas kernels: 313 us -> 297 us
  local copies, waits for them, and re-layouts: 9.24 us -> 1.77 us
    pallas_call x1, Pallas kernels: 313 us -> 297 us  [whole_slot_plan(): pl.pallas_call(expert_kernel, out_shape=jax.ShapeDtypeStruct((rows, width...]
    reshape x3 -> x0, local copies, waits for them, and re-layouts: 3.96 us -> none  [the longest x1 1.38 us: whole_slot_plan(): keep.reshape(rows, 1)]
    unnamed x3 -> x1, local copies, waits for them, and re-layouts: 5.27 us -> 1.77 us
where the time goes in v3:
time: 299 us
  Pallas kernels  297 us (99%)
    pallas_call x1, Pallas kernels, whole_slot_plan(): pl.pallas_call(expert_kernel, out_shape=jax.ShapeDtypeStruct((rows, width...  297 us

profile of v3, /device:TPU:0, one launch (start us, length us, event | category | flops | bytes accessed | tf_op | source)
XLA Modules:
  0.0 299.0 jit_solution(2428652995615897358)
XLA Ops:
  0.0 297.2 %shard_map.118 = bf16[128,1536]{1,0:T(8,128)(2,1)} custom-call(bf16[128,1536]{1,0:T(8,128)(2,1)} %attn_ref.1, bf16[128,1536]{1,0:T(8,128)(2,1)} %resid_ref.1, f32[1536]{0:T(1024)} %gain1_ref.1, f32[1536]{0:T(1024)} %gain2_ref.1, f32[40,1536]{1,0:T(8,128)} %bitcast.4, s32[8,128]{1,0:T(8,128)} %bitcast.5, s32[1,64]{1,0:T(1,128)} %bitcast.6, s32[1,128]{1,0:T(1,128)} %bitcast.7, ...), custom_call_target="tpu_custom_call" | custom-call | flops 38654705664 | bytes 9437184 | tf_op jit(solution)/shard_map/pallas_call | solution.py:421
  297.2 1.8 copy.14

commit v4 on v3

--- a/solution.py
+++ b/solution.py
@@ -304,7 +304,7 @@
         if s == 0:
             for r in (1, 3, 2):
                 send_down(r)
-        lax.fori_loop(0, 8, expert_rows, 0)
+        lax.fori_loop(0, 8, expert_rows, 0, unroll=2)
 
     def weighted(r):
         column = turned(b, r)
@@ -323,7 +323,7 @@
 
         if r:
             later[r].wait_recv()
-        lax.fori_loop(0, 8, down_rows, 0)
+        lax.fori_loop(0, 8, down_rows, 0, unroll=2)
 
     def add(r, i, j, got):
         sums[r, core, i, j] = (

time: 299 us -> 298 us (level)
  no operation moved by 1% of the time
where the time goes in v4:
time: 298 us
  Pallas kernels  296 us (99%)
    pallas_call x1, Pallas kernels, whole_slot_plan(): pl.pallas_call(expert_kernel, out_shape=jax.ShapeDtypeStruct((rows, width...  296 us

profile of v4, /device:TPU:0, one launch (start us, length us, event | category | flops | bytes accessed | tf_op | source)
XLA Modules:
  0.0 298.2 jit_solution(15239703063174142363)
XLA Ops:
  0.0 296.4 %shard_map.118 = bf16[128,1536]{1,0:T(8,128)(2,1)} custom-call(bf16[128,1536]{1,0:T(8,128)(2,1)} %attn_ref.1, bf16[128,1536]{1,0:T(8,128)(2,1)} %resid_ref.1, f32[1536]{0:T(1024)} %gain1_ref.1, f32[1536]{0:T(1024)} %gain2_ref.1, f32[40,1536]{1,0:T(8,128)} %bitcast.4, s32[8,128]{1,0:T(8,128)} %bitcast.5, s32[1,64]{1,0:T(1,128)} %bitcast.6, s32[1,128]{1,0:T(1,128)} %bitcast.7, ...), custom_call_target="tpu_custom_call" | custom-call | flops 38654705664 | bytes 9437184 | tf_op jit(solution)/shard_map/pallas_call | solution.py:421
  296.4 1.8 copy.14
